TPU v7x, 32 devices: a whole 2x2x4 slice. The times are simulated.
32 devices in a mesh: rows: 8 (over z, y), freq: 4 (over x, core).
Axes of the slice: x: 2, y: 2, z: 4, core: 2. Of those that a mesh axis runs over, the one named last changes fastest.
Arguments:
- snapshots: bfloat16 [131072, 512], P('rows', 'freq'), may hold values from -60 to 60
- block_cols: int32 [1024, 3], P('rows'), may hold values from 0 to 1023, as said below
- mass_blocks: bfloat16 [1024, 3, 128, 128], P('rows'), may hold values from -2 to 2
- start_group: float32 [512, 32], P('freq'), may hold values from -6 to 6
- start_merge: float32 [64, 32], replicated, may hold values from -6 to 6
Outputs:
- modes: float32 [32, 131072], P(None, ('rows', 'freq'))
Inputs may be any that keep to these rules, and one draw needn't show every extreme that they name: block_cols[b, 0] is b; the other entries lie within 2 of b, differ from b, and may repeat near the ends.
All inputs are finite; a program needn't handle non-finite values.
Results may differ from a plain program's by a relative error of at most 0.0003.
Values may be sent and summed in bfloat16 or wider, within the bound.
A program may use at most 128 MiB of HBM per device.

v0:
```python
import functools

import jax
import jax.numpy as jnp
from jax import lax
from jax.experimental import pallas as pl
from jax.experimental.pallas import tpu as pltpu
from jax.sharding import PartitionSpec as P

HB = 2
POWER = 2
RANK = 32
LANES = 128
STEP = 4
PIECES = 4
MASS_PIECES = 4
HIGHEST = lax.Precision.HIGHEST
MESH = pl.DeviceIdType.MESH
TRANS_B = (((1,), (1,)), ((), ()))
TRANS_A = (((0,), (0,)), ((), ()))


def dot32(a, b):
    return jnp.dot(a, b, precision=HIGHEST, preferred_element_type=jnp.float32)


def dot32_tb(a, b):
    return lax.dot_general(a, b, TRANS_B, precision=HIGHEST, preferred_element_type=jnp.float32)


def split(a):
    high = a.astype(jnp.bfloat16)
    return high, (a - high.astype(jnp.float32)).astype(jnp.bfloat16)


def pad_rows(a):
    return jnp.concatenate([a, jnp.zeros((LANES - a.shape[0], a.shape[1]), a.dtype)], axis=0)


def orthonormal_all(tops):
    row = lax.broadcasted_iota(jnp.int32, (8, LANES), 0)
    lane = lax.broadcasted_iota(jnp.int32, (8, LANES), 1)
    grams = [dot32_tb(top, pad_rows(top)) for top in tops]
    nblk = RANK // 8
    left = [[g[8 * i:8 * i + 8] for i in range(nblk)] for g in grams]
    right = [[t[8 * i:8 * i + 8] for i in range(nblk)] for t in tops]
    for j in range(RANK):
        blk, sub = j // 8, j % 8
        for a, u in zip(left, right):
            pivot_a = a[blk][sub:sub + 1]
            pivot_u = u[blk][sub:sub + 1]
            inverse = 1.0 / pivot_a[:, j:j + 1]
            scaled_a = pivot_a * inverse
            scaled_u = pivot_u * inverse
            for i in range(blk, nblk):
                column = a[i][:, j:j + 1]
                if i == blk:
                    column = jnp.where(row[:, :1] > sub, column, 0.0)
                a[i] = a[i] - column * scaled_a
                u[i] = u[i] - column * scaled_u
    outs = []
    for a, u in zip(left, right):
        done = []
        for i in range(nblk):
            diagonal = jnp.sum(jnp.where(lane == row + 8 * i, a[i], 0.0), axis=1, keepdims=True)
            done.append(u[i] * lax.rsqrt(diagonal))
        outs.append(jnp.concatenate(done, axis=0))
    return outs


def subspace_all(grams, starts):
    def body(_, tops):
        return tuple(orthonormal_all([dot32(t, g()) for t, g in zip(tops, grams)]))

    return lax.fori_loop(0, POWER, body, tuple(starts))


def kernel(
    row_count, freq_count, total_rows,
    snap, cols, mass, start_group, start_merge, out,
    x0, x1, mb, wh, wl, acc, gown, gin, rs, gfull, tbuf, starts, cbuf, sbuf, dbuf, hbuf, xr, xf,
    msem, lsem, xsend, xrecv, ssem, esem, rs_s, rs_r, ag_s, ag_r, fsem, psem_s, psem_r, dsem,
    xr_s, xr_r, xf_s, xf_r,
):
    r = lax.axis_index("rows")
    f = lax.axis_index("freq")
    c = lax.rem(f, 2)
    x = f // 2
    f_pair = f + 1 - 2 * c
    f_far = lax.rem(f + 2, 4)
    chunk = x0.shape[1] - 2 * HB
    blocks = snap.shape[0]
    size = snap.shape[1]
    xs = (x0, x1)

    def dev(rr, ff):
        return {"rows": rr, "freq": ff}

    def remote(src, dst, s_sem, r_sem, rr, ff):
        return pltpu.make_async_remote_copy(
            src_ref=src, dst_ref=dst, send_sem=s_sem, recv_sem=r_sem,
            device_id=dev(rr, ff), device_id_type=MESH,
        )

    mper = chunk // MASS_PIECES

    def mass_copy(q, p):
        base = (2 * q + c) * chunk + p * mper
        return pltpu.make_async_copy(
            mass.at[pl.ds(base, mper)], mb.at[q, pl.ds(p * mper, mper)], msem.at[q, p]
        )

    def main_range(q, d):
        return pl.ds((2 * q + d) * chunk - (HB if q else 0), chunk + HB)

    def main_dst(q):
        return pl.ds(0 if q else HB, chunk + HB)

    def edge_src(q):
        return pl.ds(chunk - HB if q == 0 else 3 * chunk, HB)

    def edge_dst(q):
        return pl.ds(0 if q == 0 else chunk + HB, HB)

    local_main = [
        pltpu.make_async_copy(snap.at[main_range(q, c)], xs[q].at[c, main_dst(q)], lsem.at[q]) for q in range(2)
    ]
    local_edge = [
        pltpu.make_async_copy(snap.at[edge_src(q)], xs[q].at[c, edge_dst(q)], lsem.at[2 + q]) for q in range(2)
    ]
    inner_edge = [c == 1, c == 0]
    for q in range(2):
        local_main[q].start()
        pl.when(inner_edge[q])(local_edge[q].start)
        for p in range(MASS_PIECES):
            mass_copy(q, p).start()

    barrier = pltpu.get_barrier_semaphore()

    def greet(rr, ff):
        pl.semaphore_signal(barrier, inc=1, device_id=dev(rr, ff), device_id_type=MESH)

    @pl.loop(1, row_count)
    def _(j):
        greet(lax.rem(r + j, row_count), f)

    for j in range(1, freq_count):
        greet(r, lax.rem(f + j, freq_count))
    has_prev = r > 0
    has_next = r < row_count - 1
    pl.when(has_prev)(lambda: greet(r - 1, f_pair))
    pl.when(has_next)(lambda: greet(r + 1, f_pair))
    expected = (
        row_count - 1 + freq_count - 1 + has_prev.astype(jnp.int32) + has_next.astype(jnp.int32)
    )
    pl.semaphore_wait(barrier, expected)

    pair_main = [
        remote(snap.at[main_range(q, 1 - c)], xs[q].at[c, main_dst(q)], xsend.at[q], xrecv.at[q], r, f_pair)
        for q in range(2)
    ]
    pair_edge = [
        remote(snap.at[edge_src(q)], xs[q].at[c, edge_dst(q)], xsend.at[2 + q], xrecv.at[2 + q], r, f_pair)
        for q in range(2)
    ]
    low_f = 2 * x
    high_f = 2 * x + 1
    to_next = remote(
        snap.at[pl.ds(blocks - HB, HB)], x0.at[c, edge_dst(0)], xsend.at[4], xrecv.at[4 + c], r + 1, low_f
    )
    to_prev = remote(
        snap.at[pl.ds(0, HB)], x1.at[c, edge_dst(1)], xsend.at[5], xrecv.at[6 + c], r - 1, high_f
    )
    pl.when(has_next)(to_next.start)
    pl.when(has_prev)(to_prev.start)
    pl.when(c == 0)(pair_edge[0].start)
    pair_main[0].start()
    pl.when(c == 1)(pair_edge[1].start)
    pair_main[1].start()

    tbuf[...] = jnp.zeros_like(tbuf)
    tbuf[:, 0:RANK] = start_group[...]
    starts[c] = tbuf[...].T[0:RANK]
    start_copy = remote(starts.at[c], starts.at[c], ssem.at[0], ssem.at[1], r, f_pair)
    start_copy.start()

    acc[...] = jnp.zeros_like(acc)

    def wait_edge(q, h):
        remote(
            snap.at[pl.ds(0, HB)], xs[q].at[h, edge_dst(q)], xsend.at[4], xrecv.at[4 + 2 * q + h], r, f_pair
        ).wait_recv()

    for q in range(2):
        local_main[q].wait()
        pair_main[q].wait_recv()
        outer = c == (1 if q else 0)

        @pl.when(inner_edge[q])
        def _():
            local_edge[q].wait()
            pair_edge[q].wait_recv()

        @pl.when(jnp.logical_and(outer, has_next if q else has_prev))
        def _():
            wait_edge(q, 0)
            wait_edge(q, 1)

        first = (2 * q + c) * chunk
        for p in range(MASS_PIECES):
            mass_copy(q, p).wait()

            @pl.loop(0, mper // STEP)
            def _(t):
                rows_done = []
                for s in range(STEP):
                    b = p * mper + t * STEP + s
                    picks = []
                    for k in range(cols.shape[1]):
                        index = jnp.clip(cols[first + b, k] - r * blocks - first + HB, 0, chunk + 2 * HB - 1)
                        picks.append(jnp.concatenate([xs[q][0, index], xs[q][1, index]], axis=1))
                    factor = jnp.concatenate([mb[q, b, k] for k in range(cols.shape[1])], axis=1)
                    rows_done.append(
                        jnp.dot(factor, jnp.concatenate(picks, axis=0), preferred_element_type=jnp.float32)
                    )
                high, low = split(jnp.concatenate(rows_done, axis=0))
                where = pl.ds(pl.multiple_of((p * mper + t * STEP) * size, STEP * size), STEP * size)
                wh[q, where, :] = high
                wl[q, where, :] = low
                acc[...] += lax.dot_general(
                    high, jnp.concatenate([high, low], axis=1), TRANS_A, preferred_element_type=jnp.float32
                )

    width = 2 * size
    gown[...] = acc[:, 0:width] + 2.0 * acc[:, width:2 * width]
    mine = pl.ds(pl.multiple_of(c * size, size), size)
    other = pl.ds(pl.multiple_of((1 - c) * size, size), size)
    exchange = remote(gown.at[other], gin, esem.at[0], esem.at[1], r, f_pair)
    exchange.start()
    exchange.wait()
    gin[...] = gin[...] + gown[mine, :]
    piece = rs.shape[1]
    owners = size // piece

    def part(i):
        return pl.ds(pl.multiple_of(i * piece, piece), piece)

    def owned(i, action):
        if owners == row_count:
            action()
        else:
            pl.when(i < owners)(action)

    def rs_copy(slot, target):
        return remote(
            gin.at[part(lax.min(target, owners - 1))], rs.at[slot], rs_s.at[target], rs_r.at[slot], target, f
        )

    def summed(i):
        return gfull.at[pl.ds(pl.multiple_of(c * size + i * piece, piece), piece)]

    def ag_copy(source, target):
        return remote(summed(source), summed(source), ag_s.at[target], ag_r.at[source], target, f)

    @pl.loop(1, row_count)
    def _(j):
        target = lax.rem(r + j, row_count)
        owned(target, lambda: rs_copy(r, target).start())

    def reduce_own():
        rs[r] = gin[part(r), :]

        @pl.loop(1, row_count)
        def _(j):
            source = lax.rem(r + j, row_count)
            rs_copy(source, source).wait_recv()

        total = rs[0]
        for s in range(1, row_count):
            total = total + rs[s]
        gfull[pl.ds(pl.multiple_of(c * size + r * piece, piece), piece), :] = total

        @pl.loop(1, row_count)
        def _(j):
            ag_copy(r, lax.rem(r + j, row_count)).start()

    owned(r, reduce_own)

    @pl.loop(1, row_count)
    def _(j):
        source = lax.rem(r + j, row_count)
        owned(source, lambda: ag_copy(source, source).wait_recv())

    give = remote(gfull.at[mine], gfull.at[mine], fsem.at[0], fsem.at[1], r, f_pair)
    give.start()
    start_copy.wait()
    give.wait()

    scale = 0.5 / total_rows
    for i in range(2):
        for j in range(2):
            a = slice(i * size, (i + 1) * size)
            b = slice(j * size, (j + 1) * size)
            gown[a, b] = (gfull[a, b] + gfull[b, a].T) * scale

    s0, s1 = subspace_all(
        [lambda: gown[0:size, 0:size], lambda: gown[size:width, size:width]], [starts[0], starts[1]]
    )
    zero = jnp.zeros((RANK, size), jnp.float32)
    basis = pad_rows(
        jnp.concatenate([jnp.concatenate([s0, zero], axis=1), jnp.concatenate([zero, s1], axis=1)], axis=0)
    )
    hbuf[...] = dot32_tb(dot32(basis, gown[...]), basis)
    tbuf[...] = jnp.zeros_like(tbuf)
    tbuf[0:2 * RANK, 0:RANK] = start_merge[...]
    merge_start = tbuf[...].T[0:RANK]
    (sm,) = subspace_all([lambda: hbuf[...]], [merge_start])
    weights = dot32(sm, basis)
    th, tl = split(weights)
    both = jnp.concatenate([th, tl], axis=0)
    pair_rows = pl.ds(pl.multiple_of(x * RANK, RANK), RANK)
    span = chunk * size // PIECES

    def modes_of(q, p):
        at = pl.ds(p * span, span)
        full = lax.dot_general(both, wh[q, at, :], TRANS_B, preferred_element_type=jnp.float32)
        rest = lax.dot_general(th, wl[q, at, :], TRANS_B, preferred_element_type=jnp.float32)
        return full[0:RANK] + (full[RANK:2 * RANK] + rest)

    def far_copy(p):
        at = pl.ds(p * span, span)
        return remote(sbuf.at[:, at], cbuf.at[pair_rows, at], psem_s.at[p], psem_r.at[p], r, f_far)

    for p in range(PIECES):
        sbuf[:, p * span:(p + 1) * span] = modes_of(1 - x, p)
        far_copy(p).start()
    dbuf[x] = dot32_tb(dot32(sm, hbuf[...]), pad_rows(sm))
    diag_copy = remote(dbuf.at[x], dbuf.at[x], dsem.at[0], dsem.at[1], r, f_far)
    diag_copy.start()
    for p in range(PIECES):
        cbuf[pair_rows, p * span:(p + 1) * span] = modes_of(x, p)
    cross = jnp.zeros((RANK, LANES), jnp.float32)
    for p in range(PIECES):
        far_copy(p).wait_recv()
        at = slice(p * span, (p + 1) * span)
        ah, al = split(cbuf[0:RANK, at])
        bh, bl = split(cbuf[RANK:2 * RANK, at])
        full = lax.dot_general(
            jnp.concatenate([ah, al], axis=0), pad_rows(bh), TRANS_B, preferred_element_type=jnp.float32
        )
        rest = lax.dot_general(ah, pad_rows(bl), TRANS_B, preferred_element_type=jnp.float32)
        cross = cross + (full[0:RANK] + (full[RANK:2 * RANK] + rest))

    packed = cross[0:8]
    for i in range(1, RANK // 8):
        packed = packed + pltpu.roll(cross[8 * i:8 * i + 8], RANK * i, 1)
    xr[r] = packed

    def xr_copy(source, target):
        return remote(xr.at[source], xr.at[source], xr_s.at[target], xr_r.at[source], target, f)

    @pl.loop(1, row_count)
    def _(j):
        xr_copy(r, lax.rem(r + j, row_count)).start()

    @pl.loop(1, row_count)
    def _(j):
        source = lax.rem(r + j, row_count)
        xr_copy(source, source).wait_recv()

    total = xr[0]
    for s in range(1, row_count):
        total = total + xr[s]
    xf[f] = total

    def xf_copy(source, target):
        return remote(xf.at[source], xf.at[source], xf_s.at[target], xf_r.at[source], r, target)

    for j in range(1, freq_count):
        xf_copy(f, lax.rem(f + j, freq_count)).start()
    for j in range(1, freq_count):
        source = lax.rem(f + j, freq_count)
        xf_copy(source, source).wait_recv()
    total = xf[0]
    for s in range(1, freq_count):
        total = total + xf[s]
    total = total * (1.0 / total_rows)
    diag_copy.wait()

    lane8 = lax.broadcasted_iota(jnp.int32, (8, LANES), 1)
    crossed = pad_rows(
        jnp.concatenate(
            [
                jnp.where(lane8 < RANK, pltpu.roll(total, LANES - RANK * i, 1) if i else total, 0.0)
                for i in range(RANK // 8)
            ],
            axis=0,
        )
    )
    hbuf[...] = jnp.zeros_like(hbuf)
    hbuf[0:RANK] = dbuf[0] + pltpu.roll(crossed[0:RANK], RANK, 1)
    hbuf[RANK:2 * RANK] = crossed.T[0:RANK] + pltpu.roll(dbuf[1], RANK, 1)
    (final,) = subspace_all([lambda: hbuf[...]], [merge_start])
    fh, fl = split(final[:, 0:2 * RANK])
    fboth = jnp.concatenate([fh, fl], axis=0)
    for p in range(PIECES):
        at = slice(p * span, (p + 1) * span)
        ch, cl = split(cbuf[:, at])
        full = jnp.dot(fboth, ch, preferred_element_type=jnp.float32)
        rest = jnp.dot(fh, cl, preferred_element_type=jnp.float32)
        out[:, at] = full[0:RANK] + (full[RANK:2 * RANK] + rest)

    for q in range(2):
        pair_main[q].wait_send()
    pl.when(c == 0)(pair_edge[0].wait_send)
    pl.when(c == 1)(pair_edge[1].wait_send)
    pl.when(has_next)(to_next.wait_send)
    pl.when(has_prev)(to_prev.wait_send)
    for p in range(PIECES):
        far_copy(p).wait_send()

    @pl.loop(1, row_count)
    def _(j):
        target = lax.rem(r + j, row_count)
        owned(target, lambda: rs_copy(r, target).wait_send())
        owned(r, lambda: ag_copy(r, target).wait_send())
        xr_copy(r, target).wait_send()

    for j in range(1, freq_count):
        xf_copy(f, lax.rem(f + j, freq_count)).wait_send()


def shards(snapshots, block_cols, mass_blocks, start_group, start_merge):
    size = mass_blocks.shape[2]
    blocks = block_cols.shape[0]
    row_count = lax.axis_size("rows")
    freq_count = lax.axis_size("freq")
    chunk = blocks // freq_count
    total_rows = row_count * snapshots.shape[0]
    piece = max(size // row_count, 8)
    share = chunk * size
    f32, bf16 = jnp.float32, jnp.bfloat16
    dma = pltpu.SemaphoreType.DMA
    any_spec = pl.BlockSpec(memory_space=pl.ANY)
    vmem = pl.BlockSpec(memory_space=pltpu.VMEM)
    smem = pl.BlockSpec(memory_space=pltpu.SMEM)
    return pl.pallas_call(
        functools.partial(kernel, row_count, freq_count, total_rows),
        out_shape=jax.ShapeDtypeStruct((RANK, share), f32),
        in_specs=[any_spec, smem, any_spec, vmem, vmem],
        out_specs=vmem,
        scratch_shapes=[
            pltpu.VMEM((2, chunk + 2 * HB, size, size), bf16),
            pltpu.VMEM((2, chunk + 2 * HB, size, size), bf16),
            pltpu.VMEM((2, chunk) + mass_blocks.shape[1:], bf16),
            pltpu.VMEM((2, share, 2 * size), bf16),
            pltpu.VMEM((2, share, 2 * size), bf16),
            pltpu.VMEM((2 * size, 4 * size), f32),
            pltpu.VMEM((2 * size, 2 * size), f32),
            pltpu.VMEM((size, 2 * size), f32),
            pltpu.VMEM((row_count, piece, 2 * size), f32),
            pltpu.VMEM((2 * size, 2 * size), f32),
            pltpu.VMEM((LANES, LANES), f32),
            pltpu.VMEM((2, RANK, LANES), f32),
            pltpu.VMEM((2 * RANK, share), f32),
            pltpu.VMEM((RANK, share), f32),
            pltpu.VMEM((2, RANK, LANES), f32),
            pltpu.VMEM((LANES, LANES), f32),
            pltpu.VMEM((row_count, 8, LANES), f32),
            pltpu.VMEM((freq_count, 8, LANES), f32),
            dma((2, MASS_PIECES)),
            dma((4,)),
            dma((6,)),
            dma((8,)),
            dma((2,)),
            dma((2,)),
            dma((row_count,)),
            dma((row_count,)),
            dma((row_count,)),
            dma((row_count,)),
            dma((2,)),
            dma((PIECES,)),
            dma((PIECES,)),
            dma((2,)),
            dma((row_count,)),
            dma((row_count,)),
            dma((freq_count,)),
            dma((freq_count,)),
        ],
        compiler_params=pltpu.CompilerParams(
            collective_id=0, has_side_effects=True, vmem_limit_bytes=48 * 1024 * 1024
        ),
    )(snapshots.reshape(blocks, size, snapshots.shape[1]), block_cols, mass_blocks, start_group, start_merge)


def solution(mesh):
    in_specs = (
        P("rows", "freq"),
        P("rows", None),
        P("rows", None, None, None),
        P("freq", None),
        P(),
    )
    out_specs = P(None, ("rows", "freq"))
    return jax.shard_map(shards, mesh=mesh, in_specs=in_specs, out_specs=out_specs, check_vma=False)
```

profile of v0, /device:TPU:0, one launch (start us, length us, event | category | flops | bytes accessed | tf_op | source)
XLA Modules:
  0.0 79.8 jit_solution(16763313744058933143)
XLA Ops:
  0.0 0.8 copy.8.start_merge
  0.8 0.8 copy.6.cols
  1.6 0.8 %copy.7.start_group = f32[128,32]{1,0:T(8,128)S(1)} copy(f32[128,32]{0,1:T(8,128)} %param.8) | data formatting | bytes 32768 | tf_op args[3]
  2.4 0.0 copy-start
  2.4 2.2 %copy-done = bf16[16384,128]{1,0:T(8,128)(2,1)S(1)} copy-done((bf16[16384,128]{1,0:T(8,128)(2,1)S(1)}, bf16[16384,128]{1,0:T(8,128)(2,1)}, u32[]{:S(2)}) %copy-start) | copy-done | bytes 4194328
  4.6 74.4 %shard_map.55 = f32[32,4096]{1,0:T(8,128)S(1)} custom-call(bf16[128,128,128]{2,1,0:T(8,128)(2,1)S(1)} %bitcast.1, s32[128,3]{1,0:T(8,128)S(1)} %copy.6.cols, bf16[128,3,128,128]{3,2,1,0:T(8,128)(2,1)} %mass.1, f32[128,32]{1,0:T(8,128)S(1)} %copy.7.start_group, f32[64,32]{1,0:T(8,128)S(1)} %copy.8.start_merge), custom_call_target="tpu_custom_call" | custom-call | tf_op jit(solution)/shard_map/pallas_call | solution.py:447
  79.0 0.8 copy.10
Async XLA Ops:
  2.4 2.2 %copy-start = (bf16[16384,128]{1,0:T(8,128)(2,1)S(1)}, bf16[16384,128]{1,0:T(8,128)(2,1)}, u32[]{:S(2)}) copy-start(bf16[16384,128]{1,0:T(8,128)(2,1)} %param.5) | copy-start | bytes 12582916
where the time goes:
time: 80.1 us; the launch traced here: 79.8 us
  Pallas kernels  74.4 us (93%)
  local copies, waits for them, and re-layouts  5.38 us (7%)
    pallas_call x1, Pallas kernels, shards(): pl.pallas_call(functools.partial(kernel, row_count, freq_count, total_row...  74.4 us
    unnamed x6, local copies, waits for them, and re-layouts  5.38 us

commit v1 on v0

--- a/solution.py
+++ b/solution.py
@@ -12,7 +12,10 @@
 RANK = 32
 LANES = 128
 STEP = 4
+GROUP = 4
 PIECES = 4
+FAR = 2
+LEVEL = 32767.0
 MASS_PIECES = 4
 HIGHEST = lax.Precision.HIGHEST
 MESH = pl.DeviceIdType.MESH
@@ -39,30 +42,43 @@
 
 def orthonormal_all(tops):
     row = lax.broadcasted_iota(jnp.int32, (8, LANES), 0)
-    lane = lax.broadcasted_iota(jnp.int32, (8, LANES), 1)
     grams = [dot32_tb(top, pad_rows(top)) for top in tops]
     nblk = RANK // 8
     left = [[g[8 * i:8 * i + 8] for i in range(nblk)] for g in grams]
     right = [[t[8 * i:8 * i + 8] for i in range(nblk)] for t in tops]
-    for j in range(RANK):
-        blk, sub = j // 8, j % 8
-        for a, u in zip(left, right):
-            pivot_a = a[blk][sub:sub + 1]
-            pivot_u = u[blk][sub:sub + 1]
-            inverse = 1.0 / pivot_a[:, j:j + 1]
-            scaled_a = pivot_a * inverse
-            scaled_u = pivot_u * inverse
-            for i in range(blk, nblk):
-                column = a[i][:, j:j + 1]
-                if i == blk:
-                    column = jnp.where(row[:, :1] > sub, column, 0.0)
-                a[i] = a[i] - column * scaled_a
-                u[i] = u[i] - column * scaled_u
+    scales = [[[] for _ in range(nblk)] for _ in tops]
+    for base in range(0, RANK, GROUP):
+        blk = base // 8
+        spread = [
+            [
+                [jnp.broadcast_to(a[i][:, base + k:base + k + 1], (8, LANES)) for i in range(blk, nblk)]
+                for k in range(GROUP)
+            ]
+            for a in left
+        ]
+        for k in range(GROUP):
+            sub = (base + k) % 8
+            for n, (a, u, columns) in enumerate(zip(left, right, spread)):
+                pivot = jnp.broadcast_to(columns[k][0][sub:sub + 1], (8, LANES))
+                scales[n][blk].append(pivot)
+                inverse = 1.0 / pivot
+                factor = [column * inverse for column in columns[k]]
+                factor[0] = jnp.where(row > sub, factor[0], 0.0)
+                for later in range(k + 1, GROUP):
+                    entry = jnp.broadcast_to(columns[later][0][sub:sub + 1], (8, LANES))
+                    columns[later] = [col - m * entry for col, m in zip(columns[later], factor)]
+                pivot_a = jnp.broadcast_to(a[blk][sub:sub + 1], (8, LANES))
+                pivot_u = jnp.broadcast_to(u[blk][sub:sub + 1], (8, LANES))
+                for i in range(blk, nblk):
+                    a[i] = a[i] - factor[i - blk] * pivot_a
+                    u[i] = u[i] - factor[i - blk] * pivot_u
     outs = []
-    for a, u in zip(left, right):
+    for u, pivots in zip(right, scales):
         done = []
         for i in range(nblk):
-            diagonal = jnp.sum(jnp.where(lane == row + 8 * i, a[i], 0.0), axis=1, keepdims=True)
+            diagonal = pivots[i][0]
+            for sub in range(1, 8):
+                diagonal = jnp.where(row == sub, pivots[i][sub], diagonal)
             done.append(u[i] * lax.rsqrt(diagonal))
         outs.append(jnp.concatenate(done, axis=0))
     return outs
@@ -78,8 +94,8 @@
 def kernel(
     row_count, freq_count, total_rows,
     snap, cols, mass, start_group, start_merge, out,
-    x0, x1, mb, wh, wl, acc, gown, gin, rs, gfull, tbuf, starts, cbuf, sbuf, dbuf, hbuf, xr, xf,
-    msem, lsem, xsend, xrecv, ssem, esem, rs_s, rs_r, ag_s, ag_r, fsem, psem_s, psem_r, dsem,
+    x0, x1, mb, wh, wl, acc, gown, rs, gfull, tbuf, starts, cbuf, qsend, qrecv, ssend, srecv, dbuf, hbuf, xr, xf,
+    msem, lsem, xsend, xrecv, ssem, rs_s, rs_r, ag_s, ag_r, psem_s, psem_r, dsem,
     xr_s, xr_r, xf_s, xf_r,
 ):
     r = lax.axis_index("rows")
@@ -140,20 +156,21 @@
     def greet(rr, ff):
         pl.semaphore_signal(barrier, inc=1, device_id=dev(rr, ff), device_id_type=MESH)
 
-    @pl.loop(1, row_count)
-    def _(j):
-        greet(lax.rem(r + j, row_count), f)
-
-    for j in range(1, freq_count):
-        greet(r, lax.rem(f + j, freq_count))
+    members = 2 * row_count
+    me = 2 * r + c
+
+    def member(i):
+        return i // 2, 2 * x + lax.rem(i, 2)
+
+    @pl.loop(1, members)
+    def _(j):
+        greet(*member(lax.rem(me + j, members)))
+
+    greet(r, f_far)
+    greet(r, lax.rem(f_pair + 2, freq_count))
     has_prev = r > 0
     has_next = r < row_count - 1
-    pl.when(has_prev)(lambda: greet(r - 1, f_pair))
-    pl.when(has_next)(lambda: greet(r + 1, f_pair))
-    expected = (
-        row_count - 1 + freq_count - 1 + has_prev.astype(jnp.int32) + has_next.astype(jnp.int32)
-    )
-    pl.semaphore_wait(barrier, expected)
+    pl.semaphore_wait(barrier, members + 1)
 
     pair_main = [
         remote(snap.at[main_range(q, 1 - c)], xs[q].at[c, main_dst(q)], xsend.at[q], xrecv.at[q], r, f_pair)
@@ -178,9 +195,7 @@
     pl.when(c == 1)(pair_edge[1].start)
     pair_main[1].start()
 
-    tbuf[...] = jnp.zeros_like(tbuf)
-    tbuf[:, 0:RANK] = start_group[...]
-    starts[c] = tbuf[...].T[0:RANK]
+    starts[c] = start_group[...]
     start_copy = remote(starts.at[c], starts.at[c], ssem.at[0], ssem.at[1], r, f_pair)
     start_copy.start()
 
@@ -207,19 +222,18 @@
             wait_edge(q, 1)
 
         first = (2 * q + c) * chunk
-        for p in range(MASS_PIECES):
+        @pl.loop(0, MASS_PIECES)
+        def _(p):
             mass_copy(q, p).wait()
-
-            @pl.loop(0, mper // STEP)
-            def _(t):
+            for t in range(mper // STEP):
                 rows_done = []
                 for s in range(STEP):
                     b = p * mper + t * STEP + s
                     picks = []
-                    for k in range(cols.shape[1]):
-                        index = jnp.clip(cols[first + b, k] - r * blocks - first + HB, 0, chunk + 2 * HB - 1)
+                    for k in range(cols.shape[0]):
+                        index = jnp.clip(cols[k, first + b] - r * blocks - first + HB, 0, chunk + 2 * HB - 1)
                         picks.append(jnp.concatenate([xs[q][0, index], xs[q][1, index]], axis=1))
-                    factor = jnp.concatenate([mb[q, b, k] for k in range(cols.shape[1])], axis=1)
+                    factor = jnp.concatenate([mb[q, b, k] for k in range(cols.shape[0])], axis=1)
                     rows_done.append(
                         jnp.dot(factor, jnp.concatenate(picks, axis=0), preferred_element_type=jnp.float32)
                     )
@@ -233,68 +247,57 @@
 
     width = 2 * size
     gown[...] = acc[:, 0:width] + 2.0 * acc[:, width:2 * width]
-    mine = pl.ds(pl.multiple_of(c * size, size), size)
-    other = pl.ds(pl.multiple_of((1 - c) * size, size), size)
-    exchange = remote(gown.at[other], gin, esem.at[0], esem.at[1], r, f_pair)
-    exchange.start()
-    exchange.wait()
-    gin[...] = gin[...] + gown[mine, :]
     piece = rs.shape[1]
-    owners = size // piece
+    owners = width // piece
 
     def part(i):
         return pl.ds(pl.multiple_of(i * piece, piece), piece)
 
     def owned(i, action):
-        if owners == row_count:
+        if owners == members:
             action()
         else:
             pl.when(i < owners)(action)
 
     def rs_copy(slot, target):
         return remote(
-            gin.at[part(lax.min(target, owners - 1))], rs.at[slot], rs_s.at[target], rs_r.at[slot], target, f
+            gown.at[part(lax.min(target, owners - 1))], rs.at[slot], rs_s.at[target], rs_r.at[slot], *member(target)
         )
 
-    def summed(i):
-        return gfull.at[pl.ds(pl.multiple_of(c * size + i * piece, piece), piece)]
-
     def ag_copy(source, target):
-        return remote(summed(source), summed(source), ag_s.at[target], ag_r.at[source], target, f)
-
-    @pl.loop(1, row_count)
-    def _(j):
-        target = lax.rem(r + j, row_count)
-        owned(target, lambda: rs_copy(r, target).start())
+        at = gfull.at[part(lax.min(source, owners - 1))]
+        return remote(at, at, ag_s.at[target], ag_r.at[source], *member(target))
+
+    @pl.loop(1, members)
+    def _(j):
+        target = lax.rem(me + j, members)
+        owned(target, lambda: rs_copy(me, target).start())
 
     def reduce_own():
-        rs[r] = gin[part(r), :]
-
-        @pl.loop(1, row_count)
+        rs[me] = gown[part(me), :]
+
+        @pl.loop(1, members)
         def _(j):
-            source = lax.rem(r + j, row_count)
+            source = lax.rem(me + j, members)
             rs_copy(source, source).wait_recv()
 
         total = rs[0]
-        for s in range(1, row_count):
+        for s in range(1, members):
             total = total + rs[s]
-        gfull[pl.ds(pl.multiple_of(c * size + r * piece, piece), piece), :] = total
-
-        @pl.loop(1, row_count)
+        gfull[part(me), :] = total
+
+        @pl.loop(1, members)
         def _(j):
-            ag_copy(r, lax.rem(r + j, row_count)).start()
-
-    owned(r, reduce_own)
-
-    @pl.loop(1, row_count)
-    def _(j):
-        source = lax.rem(r + j, row_count)
+            ag_copy(me, lax.rem(me + j, members)).start()
+
+    owned(me, reduce_own)
+    start_copy.wait()
+
+    @pl.loop(1, members)
+    def _(j):
+        source = lax.rem(me + j, members)
         owned(source, lambda: ag_copy(source, source).wait_recv())
-
-    give = remote(gfull.at[mine], gfull.at[mine], fsem.at[0], fsem.at[1], r, f_pair)
-    give.start()
-    start_copy.wait()
-    give.wait()
+        owned(source, lambda: rs_copy(me, source).wait_send())
 
     scale = 0.5 / total_rows
     for i in range(2):
@@ -312,8 +315,8 @@
     )
     hbuf[...] = dot32_tb(dot32(basis, gown[...]), basis)
     tbuf[...] = jnp.zeros_like(tbuf)
-    tbuf[0:2 * RANK, 0:RANK] = start_merge[...]
-    merge_start = tbuf[...].T[0:RANK]
+    tbuf[:, 0:2 * RANK] = start_merge[...]
+    merge_start = tbuf[...]
     (sm,) = subspace_all([lambda: hbuf[...]], [merge_start])
     weights = dot32(sm, basis)
     th, tl = split(weights)
@@ -327,22 +330,45 @@
         rest = lax.dot_general(th, wl[q, at, :], TRANS_B, preferred_element_type=jnp.float32)
         return full[0:RANK] + (full[RANK:2 * RANK] + rest)
 
-    def far_copy(p):
-        at = pl.ds(p * span, span)
-        return remote(sbuf.at[:, at], cbuf.at[pair_rows, at], psem_s.at[p], psem_r.at[p], r, f_far)
-
-    for p in range(PIECES):
-        sbuf[:, p * span:(p + 1) * span] = modes_of(1 - x, p)
-        far_copy(p).start()
+    half = chunk * size // FAR
+    tiles = half // LANES
+
+    def far_copies(p):
+        at = pl.ds(p * half, half)
+        return (
+            remote(qsend.at[:, at], qrecv.at[:, at], psem_s.at[p], psem_r.at[p], r, f_far),
+            remote(ssend.at[p], srecv.at[p], psem_s.at[FAR + p], psem_r.at[FAR + p], r, f_far),
+        )
+
+    per_half = PIECES // FAR
+    for p in range(FAR):
+        parts = [modes_of(1 - x, p * per_half + i) for i in range(per_half)]
+        cuts = [v[:, LANES * t:LANES * (t + 1)] for v in parts for t in range(span // LANES)]
+        largest = jnp.full((RANK, LANES), 1e-30, jnp.float32)
+        for v in cuts:
+            largest = jnp.maximum(largest, jnp.abs(v))
+        inverse = LEVEL / largest
+        ssend[p] = largest * (1.0 / LEVEL)
+        for t in range(tiles):
+            at = slice(p * half + t * LANES, p * half + (t + 1) * LANES)
+            qsend[:, at] = jnp.round(cuts[t] * inverse).astype(jnp.int32).astype(jnp.int16)
+        for copy in far_copies(p):
+            copy.start()
     dbuf[x] = dot32_tb(dot32(sm, hbuf[...]), pad_rows(sm))
     diag_copy = remote(dbuf.at[x], dbuf.at[x], dsem.at[0], dsem.at[1], r, f_far)
     diag_copy.start()
     for p in range(PIECES):
         cbuf[pair_rows, p * span:(p + 1) * span] = modes_of(x, p)
+    far_rows = pl.ds(pl.multiple_of((1 - x) * RANK, RANK), RANK)
     cross = jnp.zeros((RANK, LANES), jnp.float32)
-    for p in range(PIECES):
-        far_copy(p).wait_recv()
-        at = slice(p * span, (p + 1) * span)
+    for p in range(FAR):
+        for copy in far_copies(p):
+            copy.wait_recv()
+        unit = srecv[p]
+        for t in range(tiles):
+            at = slice(p * half + t * LANES, p * half + (t + 1) * LANES)
+            cbuf[far_rows, at] = qrecv[:, at].astype(jnp.int32).astype(jnp.float32) * unit
+        at = slice(p * half, (p + 1) * half)
         ah, al = split(cbuf[0:RANK, at])
         bh, bl = split(cbuf[RANK:2 * RANK, at])
         full = lax.dot_general(
@@ -416,15 +442,17 @@
     pl.when(c == 1)(pair_edge[1].wait_send)
     pl.when(has_next)(to_next.wait_send)
     pl.when(has_prev)(to_prev.wait_send)
-    for p in range(PIECES):
-        far_copy(p).wait_send()
+    for p in range(FAR):
+        for copy in far_copies(p):
+            copy.wait_send()
 
     @pl.loop(1, row_count)
     def _(j):
-        target = lax.rem(r + j, row_count)
-        owned(target, lambda: rs_copy(r, target).wait_send())
-        owned(r, lambda: ag_copy(r, target).wait_send())
-        xr_copy(r, target).wait_send()
+        xr_copy(r, lax.rem(r + j, row_count)).wait_send()
+
+    @pl.loop(1, members)
+    def _(j):
+        owned(me, lambda: ag_copy(me, lax.rem(me + j, members)).wait_send())
 
     for j in range(1, freq_count):
         xf_copy(f, lax.rem(f + j, freq_count)).wait_send()
@@ -457,13 +485,15 @@
             pltpu.VMEM((2, share, 2 * size), bf16),
             pltpu.VMEM((2 * size, 4 * size), f32),
             pltpu.VMEM((2 * size, 2 * size), f32),
-            pltpu.VMEM((size, 2 * size), f32),
-            pltpu.VMEM((row_count, piece, 2 * size), f32),
+            pltpu.VMEM((2 * row_count, piece, 2 * size), f32),
             pltpu.VMEM((2 * size, 2 * size), f32),
-            pltpu.VMEM((LANES, LANES), f32),
+            pltpu.VMEM((RANK, LANES), f32),
             pltpu.VMEM((2, RANK, LANES), f32),
             pltpu.VMEM((2 * RANK, share), f32),
-            pltpu.VMEM((RANK, share), f32),
+            pltpu.VMEM((RANK, share), jnp.int16),
+            pltpu.VMEM((RANK, share), jnp.int16),
+            pltpu.VMEM((FAR, RANK, LANES), f32),
+            pltpu.VMEM((FAR, RANK, LANES), f32),
             pltpu.VMEM((2, RANK, LANES), f32),
             pltpu.VMEM((LANES, LANES), f32),
             pltpu.VMEM((row_count, 8, LANES), f32),
@@ -473,14 +503,12 @@
             dma((6,)),
             dma((8,)),
             dma((2,)),
-            dma((2,)),
-            dma((row_count,)),
-            dma((row_count,)),
-            dma((row_count,)),
-            dma((row_count,)),
-            dma((2,)),
-            dma((PIECES,)),
-            dma((PIECES,)),
+            dma((2 * row_count,)),
+            dma((2 * row_count,)),
+            dma((2 * row_count,)),
+            dma((2 * row_count,)),
+            dma((2 * FAR,)),
+            dma((2 * FAR,)),
             dma((2,)),
             dma((row_count,)),
             dma((row_count,)),
@@ -488,9 +516,9 @@
             dma((freq_count,)),
         ],
         compiler_params=pltpu.CompilerParams(
-            collective_id=0, has_side_effects=True, vmem_limit_bytes=48 * 1024 * 1024
+            collective_id=0, has_side_effects=True, vmem_limit_bytes=51 * 1024 * 1024
         ),
-    )(snapshots.reshape(blocks, size, snapshots.shape[1]), block_cols, mass_blocks, start_group, start_merge)
+    )(snapshots.reshape(blocks, size, snapshots.shape[1]), block_cols.T, mass_blocks, start_group.T, start_merge.T)
 
 
 def solution(mesh):

time: 80.1 us -> 64.8 us (0.81)
  Pallas kernels: 74.4 us -> 61.6 us
  local copies, waits for them, and re-layouts: 5.38 us -> 2.91 us
    pallas_call x1, Pallas kernels: 74.4 us -> 61.6 us  [shards(): pl.pallas_call(functools.partial(kernel, row_count, freq_count, total_row...]
    unnamed x6 -> x7, local copies, waits for them, and re-layouts: 5.38 us -> 2.91 us
where the time goes in v1:
time: 64.8 us; the launch traced here: 64.5 us
  Pallas kernels  61.6 us (95%)
  local copies, waits for them, and re-layouts  2.91 us (4%)
    pallas_call x1, Pallas kernels, shards(): pl.pallas_call(functools.partial(kernel, row_count, freq_count, total_row...  61.6 us
    unnamed x7, local copies, waits for them, and re-layouts  2.91 us

profile of v1, /device:TPU:0, one launch (start us, length us, event | category | flops | bytes accessed | tf_op | source)
XLA Modules:
  0.0 64.5 jit_solution(13581994312938789674)
XLA Ops:
  0.0 0.0 copy-start
  0.0 0.7 %copy-done = f32[128,32]{0,1:T(8,128)S(1)} copy-done((f32[128,32]{0,1:T(8,128)S(1)}, f32[128,32]{0,1:T(8,128)}, u32[]{:S(2)}) %copy-start) | copy-done | bytes 16408
  0.7 0.0 copy-start.1
  0.7 0.7 %copy-done.1 = f32[64,32]{0,1:T(8,128)S(1)} copy-done((f32[64,32]{0,1:T(8,128)S(1)}, f32[64,32]{0,1:T(8,128)}, u32[]{:S(2)}) %copy-start.1) | copy-done | bytes 8216
  1.4 0.0 copy-start.2
  1.4 0.7 %copy-done.2 = s32[128,3]{0,1:T(4,128)S(1)} copy-done((s32[128,3]{0,1:T(4,128)S(1)}, s32[128,3]{0,1:T(4,128)}, u32[]{:S(2)}) %copy-start.2) | copy-done | bytes 1560
  2.1 61.6 %shard_map.55 = f32[32,4096]{1,0:T(8,128)S(1)} custom-call(bf16[128,128,128]{2,1,0:T(8,128)(2,1)} %bitcast.7, s32[3,128]{1,0:T(4,128)S(1)} %bitcast.6, bf16[128,3,128,128]{3,2,1,0:T(8,128)(2,1)} %mass.1, f32[32,128]{1,0:T(8,128)S(1)} %bitcast.4, f32[32,64]{1,0:T(8,128)S(1)} %bitcast.5), custom_call_target="tpu_custom_call" | custom-call | tf_op jit(solution)/shard_map/pallas_call | solution.py:475
  63.7 0.8 %copy.7 = f32[32,4096]{1,0:T(8,128)} copy(f32[32,4096]{1,0:T(8,128)S(1)} %shard_map.55) | data formatting | bytes 1048576
Async XLA Ops:
  0.0 0.7 %copy-start = (f32[128,32]{0,1:T(8,128)S(1)}, f32[128,32]{0,1:T(8,128)}, u32[]{:S(2)}) copy-start(f32[128,32]{0,1:T(8,128)} %param.8) | copy-start | bytes 49156
  0.7 0.7 %copy-start.1 = (f32[64,32]{0,1:T(8,128)S(1)}, f32[64,32]{0,1:T(8,128)}, u32[]{:S(2)}) copy-start(f32[64,32]{0,1:T(8,128)} %param.9) | copy-start | bytes 24580
  1.4 0.7 %copy-start.2 = (s32[128,3]{0,1:T(4,128)S(1)}, s32[128,3]{0,1:T(4,128)}, u32[]{:S(2)}) copy-start(s32[128,3]{0,1:T(4,128)} %param.6) | copy-start | bytes 4612

commit v2 on v1

--- a/solution.py
+++ b/solution.py
@@ -12,7 +12,7 @@
 RANK = 32
 LANES = 128
 STEP = 4
-GROUP = 4
+GROUP = 8
 PIECES = 4
 FAR = 2
 LEVEL = 32767.0
@@ -516,7 +516,7 @@
             dma((freq_count,)),
         ],
         compiler_params=pltpu.CompilerParams(
-            collective_id=0, has_side_effects=True, vmem_limit_bytes=51 * 1024 * 1024
+            collective_id=0, has_side_effects=True, vmem_limit_bytes=56 * 1024 * 1024
         ),
     )(snapshots.reshape(blocks, size, snapshots.shape[1]), block_cols.T, mass_blocks, start_group.T, start_merge.T)
 

time: 64.8 us -> 61.9 us (0.955)
  Pallas kernels: 61.6 us -> 59.7 us
  local copies, waits for them, and re-layouts: 2.91 us -> 1.87 us
    pallas_call x1, Pallas kernels: 61.6 us -> 59.7 us  [shards(): pl.pallas_call(functools.partial(kernel, row_count, freq_count, total_row...]
    unnamed x7 -> x1, local copies, waits for them, and re-layouts: 2.91 us -> 1.87 us
where the time goes in v2:
time: 61.9 us; the launch traced here: 61.6 us
  Pallas kernels  59.7 us (96%)
  local copies, waits for them, and re-layouts  1.87 us (3%)
    pallas_call x1, Pallas kernels, shards(): pl.pallas_call(functools.partial(kernel, row_count, freq_count, total_row...  59.7 us
    unnamed x1, local copies, waits for them, and re-layouts  1.87 us

profile of v2, /device:TPU:0, one launch (start us, length us, event | category | flops | bytes accessed | tf_op | source)
XLA Modules:
  0.0 61.6 jit_solution(18027356486703102184)
XLA Ops:
  0.0 59.7 %shard_map.55 = f32[32,4096]{1,0:T(8,128)} custom-call(bf16[128,128,128]{2,1,0:T(8,128)(2,1)} %bitcast.4, s32[3,128]{1,0:T(4,128)} %bitcast.7, bf16[128,3,128,128]{3,2,1,0:T(8,128)(2,1)} %mass.1, f32[32,128]{1,0:T(8,128)} %bitcast.5, f32[32,64]{1,0:T(8,128)} %bitcast.6), custom_call_target="tpu_custom_call" | custom-call | tf_op jit(solution)/shard_map/pallas_call | solution.py:475
  59.8 1.9 %copy.7 = f32[32,4096]{1,0:T(8,128)} copy(f32[32,4096]{1,0:T(8,128)} %shard_map.55) | data formatting | bytes 1048576
